TPU v7x, 32 devices: a whole 2x2x4 slice. The times are simulated.
32 devices in a mesh: seq: 4 (over y, core), strand: 2 (over x), head: 4 (over z).
Axes of the slice: x: 2, y: 2, z: 4, core: 2. Of those that a mesh axis runs over, the one named last changes fastest.
Arguments:
- top: bfloat16 [4, 2, 1024, 1536], P('head', 'strand', 'seq'), may hold values from -6 to 6
- grad_heads: bfloat16 [4, 2, 1024, 1536], P(None, 'strand', 'seq', 'head'), may hold values from -6 to 6
- tap_weight_grid: bfloat16 [3, 768, 768], P(None, 'seq'), may hold values from -0.125 to 0.125
- out_w: bfloat16 [768, 768], P('seq'), may hold values from -0.21875 to 0.21875
- mix_w: bfloat16 [768, 768], P('seq'), may hold values from -0.21875 to 0.21875
- rc_perm: int32 [768], replicated, may hold values from 0 to 767, each once
Outputs:
- restored: bfloat16 [4, 2, 1024, 1536], P('head', 'strand', 'seq')
- grad_input: bfloat16 [4, 2, 1024, 1536], P('head', 'strand', 'seq')
Inputs may be any that keep to these rules, and one draw needn't show every extreme that they name: `rc_perm`: every channel index appears exactly once.
All inputs are finite; a program needn't handle non-finite values.
Results may differ from a plain program's by a relative error of at most 0.008.
Values may be sent and summed in bfloat16 or wider, within the bound.
A program may use at most 64 MiB of HBM per device.

v0:
```python
import jax
import jax.numpy as jnp
from jax import lax
from jax.sharding import PartitionSpec as P


def swapped(value, axis, bit):
    mask = 2**bit
    pairs = [(source, source ^ mask) for source in range(lax.axis_size(axis))]
    return lax.ppermute(value, axis, pairs)


def with_halo(array, sides, width):
    for axis, dim in sides:
        devices, length = (lax.axis_size(axis), array.shape[dim])
        up = [(i, (i + 1) % devices) for i in range(devices - 1)]
        down = [(j, i) for i, j in up]
        last = lax.slice_in_dim(array, length - width, length, axis=dim)
        first = lax.slice_in_dim(array, 0, width, axis=dim)
        before = lax.ppermute(last, axis, up)
        after = lax.ppermute(first, axis, down)
        array = jnp.concatenate([before, array, after], axis=dim)
    return array


def taps_forward(padded, kernel, length, dilation):
    total = jnp.dot(padded[0:length], kernel[0], preferred_element_type=jnp.float32)
    total = total + jnp.dot(
        padded[dilation : dilation + length], kernel[1], preferred_element_type=jnp.float32
    )
    return total + jnp.dot(
        padded[2 * dilation : 2 * dilation + length], kernel[2], preferred_element_type=jnp.float32
    )


def taps_backward(padded, kernel, length, dilation):
    total = jnp.einsum(
        "pd,cd->pc",
        padded[2 * dilation : 2 * dilation + length],
        kernel[0],
        preferred_element_type=jnp.float32,
    )
    total = total + jnp.einsum(
        "pd,cd->pc",
        padded[dilation : dilation + length],
        kernel[1],
        preferred_element_type=jnp.float32,
    )
    return total + jnp.einsum(
        "pd,cd->pc", padded[0:length], kernel[2], preferred_element_type=jnp.float32
    )


def shards(top, grad_heads, tap_weight_grid, out_w, mix_w, rc_perm):
    length = top.shape[2]
    dilation = length // 2
    half = top.shape[3] // 2
    cotan = lax.all_to_all(grad_heads, "head", split_axis=0, concat_axis=3, tiled=True)[0, 0]
    conv_full, out_full, mix_full = (
        lax.all_gather(tap_weight_grid, "seq", axis=1, tiled=True),
        lax.all_gather(out_w, "seq", axis=0, tiled=True),
        lax.all_gather(mix_w, "seq", axis=0, tiled=True),
    )
    top_a = top[0, 0, :, :half]
    top_b = top[0, 0, :, half:]
    grad_a = cotan[:, :half]
    second_gradient = cotan[:, half:]
    inverse = jnp.zeros((half,), jnp.int32).at[rc_perm].set(jnp.arange(half, dtype=jnp.int32))
    other_a = swapped(top_a, "strand", 0)
    mirror = jnp.take(other_a, rc_perm, axis=1)
    paired = (top_a.astype(jnp.float32) + mirror.astype(jnp.float32)).astype(jnp.bfloat16)
    mixing = jnp.dot(paired, mix_full, preferred_element_type=jnp.float32)
    second_input = (top_b.astype(jnp.float32) - mixing).astype(jnp.bfloat16)
    padded_b = with_halo(second_input, (("seq", 0),), dilation)
    preactivation_rows = taps_forward(padded_b, conv_full, length, dilation)
    hidden = jax.nn.gelu(preactivation_rows).astype(jnp.bfloat16)
    branch_out = jnp.dot(hidden, out_full, preferred_element_type=jnp.float32)
    input_a = (top_a.astype(jnp.float32) - branch_out).astype(jnp.bfloat16)
    backed = jnp.einsum(
        "pd,cd->pc", second_gradient, mix_full, preferred_element_type=jnp.float32
    ).astype(jnp.bfloat16)
    returned = swapped(jnp.take(backed, inverse, axis=1), "strand", 0)
    cot_a = (
        grad_a.astype(jnp.float32) + backed.astype(jnp.float32) + returned.astype(jnp.float32)
    ).astype(jnp.bfloat16)
    pulled = jnp.einsum("pd,cd->pc", cot_a, out_full, preferred_element_type=jnp.float32)
    unused, slope = jax.vjp(jax.nn.gelu, preactivation_rows)
    preactivation_cotangent = slope(pulled)[0].astype(jnp.bfloat16)
    padded_cot = with_halo(preactivation_cotangent, (("seq", 0),), dilation)
    cotangent_second = (
        second_gradient.astype(jnp.float32) + taps_backward(padded_cot, conv_full, length, dilation)
    ).astype(jnp.bfloat16)
    restored = jnp.concatenate([input_a, second_input], axis=1)[None, None]
    grad_input = jnp.concatenate([cot_a, cotangent_second], axis=1)[None, None]
    return (restored, grad_input)


def solution(mesh):
    placed = (
        P("head", "strand", "seq", None),
        P(None, "strand", "seq", "head"),
        P(None, "seq", None),
        P("seq", None),
        P("seq", None),
        P(),
    )
    return jax.shard_map(
        shards,
        mesh=mesh,
        in_specs=placed,
        out_specs=(P("head", "strand", "seq", None), P("head", "strand", "seq", None)),
        check_vma=False,
    )
```

profile of v0, /device:TPU:1, one launch (start us, length us, event | category | flops | bytes accessed | tf_op | source)
XLA Modules:
  0.0 102.9 jit_solution(10511111323586730585)
XLA Ops:
  7.2 0.0 all-gather.4.cloned.1.call-start
  7.2 0.7 all-gather.4.cloned.1.call-update
  7.9 0.0 copy-start.8
  7.9 0.0 all-gather.6.cloned.1.call-start
  8.0 0.7 all-gather.6.cloned.1.call-update
  8.7 5.4 %all-to-all-start = ((bf16[4,1,256,384]{3,2,1,0:T(8,128)(2,1)}), bf16[4,1,256,384]{3,2,1,0:T(8,128)(2,1)S(1)}, u32[]{:S(2)}, u32[]{:S(2)}) async-start(bf16[4,1,256,384]{3,2,1,0:T(8,128)(2,1)} %param.9), calls=%async_computation | async-start | bytes 1572864 | tf_op jit(solution)/shard_map/all_to_all | solution.py:58
  14.1 1.3 %collective-permute-start = (bf16[256,768]{1,0:T(8,128)(2,1)S(1)}, bf16[256,768]{1,0:T(8,128)(2,1)S(1)}, u32[]{:S(2)}, u32[]{:S(2)}) collective-permute-start(bf16[256,768]{1,0:T(8,128)(2,1)S(1)} %slice_bitcast_fusion.9), channel_id=1, source_target_pairs={{0,4},{4,0},{1,5},{5,1},{2,6},{6,2},{3,7},{7,3},{8,12},{12,8},{9,1... | collective-permute-start | bytes 1179656 | tf_op jit(solution)/shard_map/ppermute | solution.py:10
  15.4 0.0 all-gather.8.cloned.1.call-update
  15.5 3.4 %scatter_custom_fusion = s32[768]{0:T(1024)S(1)} fusion(s32[768]{0:T(1024)S(1)} %compare_select_fusion.1, s32[768]{0:T(1024)S(1)} %iota.3, s32[]{:T(128)} %constant.9.clone.1), kind=kCustom, calls=%fused_computation.61 | custom fusion | bytes 3076 | tf_op jit(solution)/shard_map/scatter | solution.py:68
  18.9 5.0 %collective-permute-done = bf16[256,768]{1,0:T(8,128)(2,1)S(1)} collective-permute-done((bf16[256,768]{1,0:T(8,128)(2,1)S(1)}, bf16[256,768]{1,0:T(8,128)(2,1)S(1)}, u32[]{:S(2)}, u32[]{:S(2)}) %collective-permute-start) | collective-permute-done | bytes 393248 | tf_op jit(solution)/shard_map/ppermute | solution.py:10
  24.0 0.2 copy.8
  24.1 2.7 %gather_fusion = bf16[768,256]{1,0:T(8,128)(2,1)S(1)} fusion(bf16[256,768]{0,1:T(8,128)(2,1)S(1)} %copy.8, s32[1024]{0:T(1024)S(1)} %pad_clamp_fusion.1), kind=kCustom, calls=%fused_computation.clone | custom fusion | bytes 789504 | tf_op jit(solution)/shard_map/jit(_take)/gather | solution.py:70
  26.8 0.2 copy.9
  27.0 6.7 %all-to-all-done = bf16[4,1,256,384]{3,2,1,0:T(8,128)(2,1)S(1)} async-done(((bf16[4,1,256,384]{3,2,1,0:T(8,128)(2,1)}), bf16[4,1,256,384]{3,2,1,0:T(8,128)(2,1)S(1)}, u32[]{:S(2)}, u32[]{:S(2)}) %all-to-all-start) | async-done | bytes 786464 | tf_op jit(solution)/shard_map/all_to_all | solution.py:58
  33.7 0.6 copy.10
  34.3 0.1 copy.13
  34.5 0.0 all-gather.4.cloned.1.call-done
  34.5 2.0 %convolution_convert_fusion = bf16[256,768]{1,0:T(8,128)(2,1)S(1)} fusion(bf16[768,768]{1,0:T(8,128)(2,1)} %all-gather.4.cloned.1.call-done, bf16[256,1536]{1,0:T(8,128)(2,1)S(1)} %bitcast.49), kind=kOutput, calls=%fused_computation.13 | convolution fusion | flops 302186496 | bytes 1966080 | tf_op jit(solution)/shard_map/pd,cd->pc/dot_general | solution.py:79
  36.5 0.2 copy.11
  36.7 2.7 %gather_fusion.1 = bf16[768,256]{1,0:T(8,128)(2,1)S(1)} fusion(bf16[256,768]{0,1:T(8,128)(2,1)S(1)} %copy.11, s32[1024]{0:T(1024)S(1)} %pad_clamp_fusion), kind=kCustom, calls=%fused_computation.1.clone | custom fusion | bytes 789504 | tf_op jit(solution)/shard_map/jit(_take)/gather | solution.py:82
  39.4 0.2 copy.12
  39.6 1.3 %collective-permute-start.3 = (bf16[256,768]{1,0:T(8,128)(2,1)S(1)}, bf16[256,768]{1,0:T(8,128)(2,1)S(1)}, u32[]{:S(2)}, u32[]{:S(2)}) collective-permute-start(bf16[256,768]{1,0:T(8,128)(2,1)S(1)} %select_bitcast_fusion), channel_id=1, source_target_pairs={{0,4},{4,0},{1,5},{5,1},{2,6},{6,2},{3,7},{7,3},{8,12},{12,8},{9,1... | collective-permute-start | bytes 1179656 | tf_op jit(solution)/shard_map/ppermute | solution.py:10
  40.9 1.8 %fusion.3 = bf16[256,768]{1,0:T(8,128)(2,1)S(1)} fusion(bf16[768,768]{1,0:T(8,128)(2,1)} %all-gather.4.cloned.1.call-done, bf16[768,256]{0,1:T(8,128)(2,1)S(1)} %copy.9, bf16[1,1,256,1536]{3,2,1,0:T(8,128)(2,1)S(1)} %copy-done.8, pred[768]{0:T(1024)(128)(4,1)S(1)} %compare_and_fusion.1), kind=kOutput, calls=%fused_computation.10 | convolution fusion | flops 303562752 | bytes 2753280 | tf_op jit(solution)/shard_map/dot_general | solution.py:72
  42.6 0.0 copy-start.1
  42.6 0.7 copy-done.1
  43.4 0.8 fusion.44
  44.2 4.8 %collective-permute-start.1 = (bf16[128,768]{1,0:T(8,128)(2,1)}, bf16[128,768]{1,0:T(8,128)(2,1)}, u32[]{:S(2)}, u32[]{:S(2)}) collective-permute-start(bf16[128,768]{1,0:T(8,128)(2,1)} %get-tuple-element.5), channel_id=1, source_target_pairs={{0,8},{8,16},{16,24},{1,9},{9,17},{17,25},{2,10},{10,18},{18,26},{... | collective-permute-start | bytes 589832 | tf_op jit(solution)/shard_map/ppermute | solution.py:20
  48.9 1.9 %collective-permute-start.2 = (bf16[128,768]{1,0:T(8,128)(2,1)}, bf16[128,768]{1,0:T(8,128)(2,1)}, u32[]{:S(2)}, u32[]{:S(2)}) collective-permute-start(bf16[128,768]{1,0:T(8,128)(2,1)} %get-tuple-element.6), channel_id=1, source_target_pairs={{8,0},{16,8},{24,16},{9,1},{17,9},{25,17},{10,2},{18,10},{26,18},{... | collective-permute-start | bytes 589832 | tf_op jit(solution)/shard_map/ppermute | solution.py:21
  50.9 0.0 collective-permute-done.3
  50.9 0.9 add_convert_fusion
  51.8 12.2 %all-gather.6.cloned.1.call-done = bf16[3,768,768]{2,1,0:T(8,128)(2,1)} async-done(((bf16[3,192,768]{2,1,0:T(8,128)(2,1)}), bf16[3,768,768]{2,1,0:T(8,128)(2,1)}) %all-gather.6.cloned.1.call-update) | async-done | bytes 3538960 | tf_op jit(solution)/shard_map/all_gather | solution.py:60
  64.0 2.0 %fusion.7 = f32[256,768]{1,0:T(8,128)S(1)} fusion(bf16[256,768]{1,0:T(8,128)(2,1)} %copy-done.1, bf16[3,768,768]{2,1,0:T(8,128)(2,1)} %all-gather.6.cloned.1.call-done), kind=kOutput, calls=%fused_computation.20 | convolution fusion | flops 301989888 | bytes 2359296 | tf_op jit(solution)/shard_map/dot_general | solution.py:28
  66.0 0.0 copy-start.2
  66.1 2.0 %fusion.9 = f32[256,768]{1,0:T(8,128)S(1)} fusion(bf16[3,768,768]{2,1,0:T(8,128)(2,1)} %all-gather.6.cloned.1.call-done, bf16[128,768]{1,0:T(8,128)(2,1)} %collective-permute-done.2, bf16[256,768]{1,0:T(8,128)(2,1)} %copy-done.1), kind=kOutput, calls=%fused_computation.22 | convolution fusion | flops 302776320 | bytes 2555904 | tf_op jit(solution)/shard_map/dot_general | solution.py:31
  68.1 2.3 %fusion.2 = f32[256,768]{1,0:T(8,128)} fusion(f32[256,768]{1,0:T(8,128)S(1)} %fusion.9, f32[256,768]{1,0:T(8,128)S(1)} %fusion.7, bf16[3,768,768]{2,1,0:T(8,128)(2,1)S(1)} %copy-done, bf16[256,768]{1,0:T(8,128)(2,1)S(1)} %copy-done.2, bf16[128,768]{1,0:T(8,128)(2,1)} %collective-permute-done.1), kind=kOutput, calls=%fused_computation.8 | convolution fusion | flops 303169536 | bytes 4128768 | tf_op jit(solution)/shard_map/dot_general | solution.py:27
  70.4 12.7 %all-gather.8.cloned.1.call-done = bf16[768,768]{1,0:T(8,128)(2,1)} async-done(((bf16[192,768]{1,0:T(8,128)(2,1)}), bf16[768,768]{1,0:T(8,128)(2,1)}) %all-gather.8.cloned.1.call-update) | async-done | bytes 1179664 | tf_op jit(solution)/shard_map/all_gather | solution.py:61
  83.1 2.5 %fusion.17 = bf16[256,768]{1,0:T(8,128)(2,1)S(1)} fusion(f32[256,768]{1,0:T(8,128)} %fusion.2, bf16[256,768]{1,0:T(8,128)(2,1)} %add_convert_fusion, bf16[768,768]{1,0:T(8,128)(2,1)} %all-gather.8.cloned.1.call-done), kind=kOutput, calls=%fused_computation.31 | convolution fusion | flops 305922048 | bytes 2752512 | tf_op jit(solution)/shard_map/pd,cd->pc/dot_general | solution.py:86
  85.6 2.2 %collective-permute-start.4 = (bf16[128,768]{1,0:T(8,128)(2,1)S(1)}, bf16[128,768]{1,0:T(8,128)(2,1)S(1)}, u32[]{:S(2)}, u32[]{:S(2)}) collective-permute-start(bf16[128,768]{1,0:T(8,128)(2,1)S(1)} %get-tuple-element.3), channel_id=1, source_target_pairs={{8,0},{16,8},{24,16},{9,1},{17,9},{25,17},{10,2},{18,10},{26,18},{... | collective-permute-start | bytes 589832 | tf_op jit(solution)/shard_map/ppermute | solution.py:21
  87.8 3.4 %collective-permute-start.5 = (bf16[128,768]{1,0:T(8,128)(2,1)S(1)}, bf16[128,768]{1,0:T(8,128)(2,1)S(1)}, u32[]{:S(2)}, u32[]{:S(2)}) collective-permute-start(bf16[128,768]{1,0:T(8,128)(2,1)S(1)} %get-tuple-element.4), channel_id=1, source_target_pairs={{0,8},{8,16},{16,24},{1,9},{9,17},{17,25},{2,10},{10,18},{18,26},{... | collective-permute-start | bytes 589832 | tf_op jit(solution)/shard_map/ppermute | solution.py:20
  91.2 0.6 fusion.4
  91.9 0.0 copy-start.3
  91.9 0.5 fusion.6
  92.4 0.5 copy-done.3
  92.9 0.9 maximum_bitcast_fusion
  93.8 0.5 fusion.8
  94.3 0.6 copy-done.5
  94.9 0.5 fusion.5
  95.5 0.9 maximum_bitcast_fusion.1
  (32 shorter events, 0.2 us)
Async XLA Ops:
  7.2 27.3 %all-gather.4.cloned.1.call-start = ((), (), s32[]{:S(2)}) async-start(), calls=%async_computation.1 | async-start | bytes 1474560 | tf_op jit(solution)/shard_map/all_gather | solution.py:62
  7.9 6.2 %copy-start.8 = (bf16[1,1,256,1536]{3,2,1,0:T(8,128)(2,1)S(1)}, bf16[1,1,256,1536]{3,2,1,0:T(8,128)(2,1)}, u32[]{:S(2)}) copy-start(bf16[1,1,256,1536]{3,2,1,0:T(8,128)(2,1)} %param.8) | copy-start | bytes 2359300
  7.9 56.1 %all-gather.6.cloned.1.call-start = ((), (), s32[]{:S(2)}) async-start(), calls=%async_computation.2 | async-start | bytes 4423680 | tf_op jit(solution)/shard_map/all_gather | solution.py:60
  8.7 6.8 %copy-start.10 = (s32[768]{0:T(1024)S(1)}, s32[768]{0:T(1024)}, u32[]{:S(2)}) copy-start(s32[768]{0:T(1024)} %param.13) | copy-start | bytes 9220
  8.7 25.0 %all-to-all-start = ((bf16[4,1,256,384]{3,2,1,0:T(8,128)(2,1)}), bf16[4,1,256,384]{3,2,1,0:T(8,128)(2,1)S(1)}, u32[]{:S(2)}, u32[]{:S(2)}) async-start(bf16[4,1,256,384]{3,2,1,0:T(8,128)(2,1)} %param.9), calls=%async_computation | async-start | bytes 1572864 | tf_op jit(solution)/shard_map/all_to_all | solution.py:58
  14.1 69.0 %all-gather.8.cloned.1.call-start = ((), (), s32[]{:S(2)}) async-start(), calls=%async_computation.3 | async-start | bytes 1474560 | tf_op jit(solution)/shard_map/all_gather | solution.py:61
  14.1 9.8 %collective-permute-start = (bf16[256,768]{1,0:T(8,128)(2,1)S(1)}, bf16[256,768]{1,0:T(8,128)(2,1)S(1)}, u32[]{:S(2)}, u32[]{:S(2)}) collective-permute-start(bf16[256,768]{1,0:T(8,128)(2,1)S(1)} %slice_bitcast_fusion.9), channel_id=1, source_target_pairs={{0,4},{4,0},{1,5},{5,1},{2,6},{6,2},{3,7},{7,3},{8,12},{12,8},{9,1... | collective-permute-start | bytes 1179656 | tf_op jit(solution)/shard_map/ppermute | solution.py:10
  34.4 16.4 %copy-start.4 = (bf16[32,8,4,384]{3,1,2,0:T(8,128)(2,1)}, bf16[32,8,4,384]{3,1,2,0:T(8,128)(2,1)S(1)}, u32[]{:S(2)}) copy-start(bf16[32,8,4,384]{3,1,2,0:T(8,128)(2,1)S(1)} %copy.13) | copy-start | bytes 2359300
  39.6 11.3 %collective-permute-start.3 = (bf16[256,768]{1,0:T(8,128)(2,1)S(1)}, bf16[256,768]{1,0:T(8,128)(2,1)S(1)}, u32[]{:S(2)}, u32[]{:S(2)}) collective-permute-start(bf16[256,768]{1,0:T(8,128)(2,1)S(1)} %select_bitcast_fusion), channel_id=1, source_target_pairs={{0,4},{4,0},{1,5},{5,1},{2,6},{6,2},{3,7},{7,3},{8,12},{12,8},{9,1... | collective-permute-start | bytes 1179656 | tf_op jit(solution)/shard_map/ppermute | solution.py:10
  42.6 0.7 copy-start.1
  44.2 23.9 %collective-permute-start.1 = (bf16[128,768]{1,0:T(8,128)(2,1)}, bf16[128,768]{1,0:T(8,128)(2,1)}, u32[]{:S(2)}, u32[]{:S(2)}) collective-permute-start(bf16[128,768]{1,0:T(8,128)(2,1)} %get-tuple-element.5), channel_id=1, source_target_pairs={{0,8},{8,16},{16,24},{1,9},{9,17},{17,25},{2,10},{10,18},{18,26},{... | collective-permute-start | bytes 589832 | tf_op jit(solution)/shard_map/ppermute | solution.py:20
  48.9 17.1 %collective-permute-start.2 = (bf16[128,768]{1,0:T(8,128)(2,1)}, bf16[128,768]{1,0:T(8,128)(2,1)}, u32[]{:S(2)}, u32[]{:S(2)}) collective-permute-start(bf16[128,768]{1,0:T(8,128)(2,1)} %get-tuple-element.6), channel_id=1, source_target_pairs={{8,0},{16,8},{24,16},{9,1},{17,9},{25,17},{10,2},{18,10},{26,18},{... | collective-permute-start | bytes 589832 | tf_op jit(solution)/shard_map/ppermute | solution.py:21
  64.0 4.1 %copy-start = (bf16[3,768,768]{2,1,0:T(8,128)(2,1)S(1)}, bf16[3,768,768]{2,1,0:T(8,128)(2,1)}, u32[]{:S(2)}) copy-start(bf16[3,768,768]{2,1,0:T(8,128)(2,1)} %all-gather.6.cloned.1.call-done) | copy-start | bytes 10616836
  66.0 2.0 %copy-start.2 = (bf16[256,768]{1,0:T(8,128)(2,1)S(1)}, bf16[256,768]{1,0:T(8,128)(2,1)}, u32[]{:S(2)}) copy-start(bf16[256,768]{1,0:T(8,128)(2,1)} %copy-done.1) | copy-start | bytes 1179652
  83.1 8.1 %copy-start.7 = (f32[256,768]{1,0:T(8,128)S(1)}, f32[256,768]{1,0:T(8,128)}, u32[]{:S(2)}) copy-start(f32[256,768]{1,0:T(8,128)} %fusion.2) | copy-start | bytes 2359300
  83.1 8.1 %copy-start.9 = (bf16[1,1,256,1536]{3,2,1,0:T(8,128)(2,1)S(1)}, bf16[1,1,256,1536]{3,2,1,0:T(8,128)(2,1)}, u32[]{:S(2)}) copy-start(bf16[1,1,256,1536]{3,2,1,0:T(8,128)(2,1)} %param.8) | copy-start | bytes 2359300
  83.1 8.2 %copy-start.11 = (bf16[768,768]{1,0:T(8,128)(2,1)S(1)}, bf16[768,768]{1,0:T(8,128)(2,1)}, u32[]{:S(2)}) copy-start(bf16[768,768]{1,0:T(8,128)(2,1)} %all-gather.8.cloned.1.call-done) | copy-start | bytes 3538948
  85.6 8.7 %collective-permute-start.4 = (bf16[128,768]{1,0:T(8,128)(2,1)S(1)}, bf16[128,768]{1,0:T(8,128)(2,1)S(1)}, u32[]{:S(2)}, u32[]{:S(2)}) collective-permute-start(bf16[128,768]{1,0:T(8,128)(2,1)S(1)} %get-tuple-element.3), channel_id=1, source_target_pairs={{8,0},{16,8},{24,16},{9,1},{17,9},{25,17},{10,2},{18,10},{26,18},{... | collective-permute-start | bytes 589832 | tf_op jit(solution)/shard_map/ppermute | solution.py:21
  87.8 6.0 %collective-permute-start.5 = (bf16[128,768]{1,0:T(8,128)(2,1)S(1)}, bf16[128,768]{1,0:T(8,128)(2,1)S(1)}, u32[]{:S(2)}, u32[]{:S(2)}) collective-permute-start(bf16[128,768]{1,0:T(8,128)(2,1)S(1)} %get-tuple-element.4), channel_id=1, source_target_pairs={{0,8},{8,16},{16,24},{1,9},{9,17},{17,25},{2,10},{10,18},{18,26},{... | collective-permute-start | bytes 589832 | tf_op jit(solution)/shard_map/ppermute | solution.py:20
  91.9 1.0 copy-start.3
  93.8 1.1 %copy-start.5 = (bf16[32,8,4,384]{3,1,2,0:T(8,128)(2,1)S(1)}, bf16[32,8,4,384]{3,1,2,0:T(8,128)(2,1)}, u32[]{:S(2)}) copy-start(bf16[32,8,4,384]{3,1,2,0:T(8,128)(2,1)} %copy-done.4) | copy-start | bytes 2359300
  94.3 1.2 %copy-start.6 = (bf16[256,768]{1,0:T(8,128)(2,1)S(1)}, bf16[256,768]{1,0:T(8,128)(2,1)}, u32[]{:S(2)}) copy-start(bf16[256,768]{1,0:T(8,128)(2,1)} %add_convert_fusion) | copy-start | bytes 1179652
Sparse Core Ops, SparseCore 0:
  9.6 19.9 all-gather.3
  31.1 32.8 all-gather.5
  65.6 17.4 all-gather.7
where the time goes:
time: 103 us
  waiting for transfers between devices  38.1 us (37%)
  starting transfers between devices  20.3 us (20%)
  matrix products  14.8 us (14%)
  between operations  14.1 us (14%)
  local copies, waits for them, and re-layouts  12.8 us (12%)
  other arithmetic  2.82 us (3%)
    all_gather x1, waiting for transfers between devices, shards(): lax.all_gather(out_w, 'seq', axis=0, tiled=True)  12.7 us
    all_gather x1, waiting for transfers between devices, shards(): lax.all_gather(tap_weight_grid, 'seq', axis=1, tiled=True)  12.2 us
    ppermute x2, starting transfers between devices, with_halo(): before = lax.ppermute(last, axis, up)  8.14 us
    all_to_all x1, waiting for transfers between devices, shards(): lax.all_to_all(grad_heads, 'head', split_axis=0, concat_axis=3, tiled=True)  6.73 us
    all_to_all x1, starting transfers between devices, shards(): lax.all_to_all(grad_heads, 'head', split_axis=0, concat_axis=3, tiled=True)  5.43 us
    ppermute x2, waiting for transfers between devices, swapped(): return lax.ppermute(value, axis, pairs)  5.05 us
    ppermute x2, starting transfers between devices, with_halo(): after = lax.ppermute(first, axis, down)  4.11 us
    scatter x1, local copies, waits for them, and re-layouts, shards(): jnp.zeros((half,), jnp.int32).at[rc_perm]  3.38 us
  transfers between devices with their start and end apart: 10, of which 4 were waited for; matrix products, arithmetic and copies ran while one was open for 24% of the time, Pallas kernels for 0%

commit v1 on v0

v1 whole, which is shorter than its diff:
```python
import functools
import math

import jax
import jax.numpy as jnp
from jax import lax
from jax.experimental import pallas as pl
from jax.experimental.pallas import tpu as pltpu
from jax.sharding import PartitionSpec as P

MESH = pl.DeviceIdType.MESH
F32, BF16 = jnp.float32, jnp.bfloat16
ROUTES = ("far", "strand", "head", "head", "head")


def dot(a, b):
    return jnp.dot(a, b, preferred_element_type=F32)


def dot_t(a, b):
    return lax.dot_general(a, b, (((1,), (1,)), ((), ())), preferred_element_type=F32)


def kernel(
    n, heads, relay,
    top, grad, taps, out_w, mix_w, perm,
    restored, grad_in,
    full, onehot, topv, other, paired, cot, pad, padc, backed, back_in, pre, pulled, rest, gout,
    send, recv, local,
):
    s, x, z = lax.axis_index("seq"), lax.axis_index("strand"), lax.axis_index("head")
    length, half = other.shape
    dil = length // 2
    rows, width = mix_w.shape[0], grad.shape[3]
    started, counter, waits = [], [0], [0]

    def remote(src, dst, device):
        i = counter[0]
        counter[0] += 1
        return lambda s_ref=src, d_ref=dst: pltpu.make_async_remote_copy(
            src_ref=s_ref, dst_ref=d_ref, send_sem=send.at[i], recv_sem=recv.at[i],
            device_id=device, device_id_type=MESH)

    def start(make):
        copy = make()
        copy.start()
        started.append(copy)

    def arrived(make, ref):
        make(ref, ref).wait_recv()

    def here(src, dst):
        copy = pltpu.make_async_copy(src, dst, local.at[waits[0]])
        waits[0] += 1
        copy.start()
        return copy

    weights = [mix_w, out_w] + [taps.at[k] for k in range(taps.shape[0])]
    count = len(weights)
    top_copy = here(top.at[0, 0], topv)
    own_z = here(grad.at[z, 0], cot.at[:, pl.ds(pl.multiple_of(z * width, 128), width)])
    if relay:
        base = pl.multiple_of(s * rows, 16)
        own_w = [here(w, full.at[m, pl.ds(base, rows), :]) for m, w in enumerate(weights)]
    else:
        own_w = [here(w, full.at[m]) for m, w in enumerate(weights)]

    barrier = pltpu.get_barrier_semaphore()
    ring = range(1, n) if relay else ((1, n - 1) if n > 2 else range(1, n))
    greeted = [{"seq": lax.rem(s + i, n)} for i in ring]
    greeted += [{"strand": 1 - x}] + [{"head": lax.rem(z + i, heads)} for i in range(1, heads)]
    for device in greeted:
        pl.semaphore_signal(barrier, inc=1, device_id=device, device_id_type=MESH)
    pl.semaphore_wait(barrier, len(greeted))

    to_strand = {"strand": 1 - x}
    swap = remote(top.at[0, 0, :, pl.ds(0, half)], other, to_strand)
    start(swap)

    if relay:
        core = lax.rem(s, 2)
        sib, far = s + 1 - 2 * core, lax.rem(s + 2, n)
        sib_far = lax.rem(sib + 2, n)
        hr = rows // 2

        def seg(m, owner, first, size):
            return full.at[m, pl.ds(pl.multiple_of(owner * rows + first, 16), size), :]

        plans = []
        for m in range(count):
            turn = {"far": None, "strand": x, "head": lax.rem(z, 2)}[ROUTES[m]]
            first, size = (0, rows) if turn is None else (pl.multiple_of(turn * hr, 16), hr)
            rest_first = None if turn is None else pl.multiple_of((1 - turn) * hr, 16)
            partner = {"far": None, "strand": to_strand, "head": {"head": z + 1 - 2 * lax.rem(z, 2)}}[ROUTES[m]]
            w = weights[m]
            plan = {
                "first": first, "size": size, "rest": rest_first,
                "sib": remote(w, seg(m, s, 0, rows), {"seq": sib}),
                "far": remote(w.at[pl.ds(first, size), :], seg(m, s, first, size), {"seq": far}),
                "fwd": remote(seg(m, far, first, size), seg(m, far, first, size), {"seq": sib}),
            }
            if turn is not None:
                plan["relay"] = remote(seg(m, far, first, size), seg(m, far, first, size), partner)
                plan["fwd2"] = remote(seg(m, far, rest_first, hr), seg(m, far, rest_first, hr), {"seq": sib})
            plans.append(plan)

    def push(m):
        if relay:
            start(plans[m]["far"])
            start(plans[m]["sib"])

    def stage_a(m):
        if relay:
            p = plans[m]
            arrived(p["far"], seg(m, far, p["first"], p["size"]))
            if p["rest"] is not None:
                start(p["relay"])
            start(p["fwd"])

    def stage_b(m):
        if relay and plans[m]["rest"] is not None:
            p = plans[m]
            arrived(p["relay"], seg(m, far, p["rest"], hr))
            start(p["fwd2"])

    def stage_c(m):
        own_w[m].wait()
        if relay:
            p = plans[m]
            arrived(p["sib"], seg(m, sib, 0, rows))
            arrived(p["fwd"], seg(m, sib_far, p["first"], p["size"]))
            if p["rest"] is not None:
                arrived(p["fwd2"], seg(m, sib_far, p["rest"], hr))

    def piece(h, owner):
        return cot.at[pl.ds(h * dil, dil), pl.ds(pl.multiple_of(owner * width, 128), width)]

    gifts = []
    for h in range(2):
        gifts.append([
            remote(grad.at[lax.rem(z + i, heads), 0, pl.ds(h * dil, dil), :], piece(h, z),
                   {"head": lax.rem(z + i, heads)})
            for i in range(1, heads)])
    push(0)
    for make in gifts[0]:
        start(make)
    for m in range(1, count):
        push(m)
    for make in gifts[1]:
        start(make)

    index = lax.broadcasted_iota(jnp.int32, (half, half), 0)
    onehot[...] = jnp.where(index == perm[...], 1.0, 0.0).astype(BF16)

    @pl.when(s == 0)
    def _():
        pad[0:dil] = jnp.zeros((dil, half), BF16)
        padc[0:dil] = jnp.zeros((dil, half), BF16)

    @pl.when(s == n - 1)
    def _():
        pad[3 * dil:] = jnp.zeros((dil, half), BF16)
        padc[3 * dil:] = jnp.zeros((dil, half), BF16)

    top_copy.wait()
    arrived(swap, other)
    paired[...] = (topv[:, :half].astype(F32) + dot(other[...], onehot[...])).astype(BF16)

    def halo(buf):
        up = remote(buf.at[pl.ds(2 * dil, dil)], buf.at[pl.ds(0, dil)], {"seq": lax.rem(s + 1, n)})
        down = remote(buf.at[pl.ds(dil, dil)], buf.at[pl.ds(3 * dil, dil)], {"seq": lax.rem(s + n - 1, n)})

        @pl.when(s < n - 1)
        def _():
            up().start()

        @pl.when(s > 0)
        def _():
            down().start()

        def finish():
            @pl.when(s > 0)
            def _():
                arrived(up, buf.at[pl.ds(0, dil)])
                down().wait_send()

            @pl.when(s < n - 1)
            def _():
                arrived(down, buf.at[pl.ds(3 * dil, dil)])
                up().wait_send()

        return finish

    returns = [remote(backed.at[pl.ds(h * dil, dil)], back_in.at[pl.ds(h * dil, dil)], to_strand)
               for h in range(2)]

    def back(h):
        if h == 0:
            own_z.wait()
        for i in range(1, heads):
            arrived(gifts[h][i - 1], piece(h, lax.rem(z + heads - i, heads)))
        rows_h = slice(h * dil, (h + 1) * dil)
        backed[rows_h] = dot_t(cot[rows_h, half:], full[0]).astype(BF16)
        start(returns[h])

    stage_a(0)
    stage_a(1)
    stage_b(0)
    stage_c(0)
    input_b = (topv[:, half:].astype(F32) - dot(paired[...], full[0])).astype(BF16)
    pad[dil:3 * dil] = input_b
    rest[:, half:] = input_b
    halo_b = halo(pad)
    stores = [here(rest.at[:, pl.ds(half, half)], restored.at[0, 0, :, pl.ds(half, half)])]
    back(0)
    stage_a(2)
    stage_b(1)
    stage_c(1)
    halo_b()
    stage_a(3)
    stage_b(2)
    stage_c(2)
    pre[...] = dot(pad[0:2 * dil], full[2])
    back(1)
    stage_a(4)
    stage_b(3)
    stage_c(3)
    pre[...] += dot(pad[dil:3 * dil], full[3])

    for h in range(2):
        rows_h = slice(h * dil, (h + 1) * dil)
        arrived(returns[h], back_in.at[pl.ds(h * dil, dil)])
        returned = dot_t(back_in[rows_h], onehot[...])
        cot_a = (cot[rows_h, :half].astype(F32) + backed[rows_h].astype(F32) + returned).astype(BF16)
        gout[rows_h, :half] = cot_a
        pulled[rows_h] = dot_t(cot_a, full[1])
    stores.append(here(gout.at[:, pl.ds(0, half)], grad_in.at[0, 0, :, pl.ds(0, half)]))

    stage_b(4)
    stage_c(4)
    scale = math.sqrt(2.0 / math.pi)
    for h in range(2):
        rows_h = slice(h * dil, (h + 1) * dil)
        v = pre[rows_h] + dot(pad[(2 + h) * dil:(3 + h) * dil], full[4])
        square = v * v
        t = jnp.tanh(scale * (v + 0.044715 * (square * v)))
        cdf = 0.5 * (1.0 + t)
        slope = cdf + 0.5 * v * (1.0 - t * t) * (scale * (1.0 + 3 * 0.044715 * square))
        padc[(1 + h) * dil:(2 + h) * dil] = (pulled[rows_h] * slope).astype(BF16)
        paired[rows_h] = (v * cdf).astype(BF16)
    halo_c = halo(padc)
    rest[:, :half] = (topv[:, :half].astype(F32) - dot(paired[...], full[1])).astype(BF16)
    stores.append(here(rest.at[:, pl.ds(0, half)], restored.at[0, 0, :, pl.ds(0, half)]))
    total = cot[:, half:].astype(F32) + dot_t(padc[dil:3 * dil], full[3])
    low = total[:dil] + dot_t(padc[2 * dil:3 * dil], full[2])
    high = total[dil:] + dot_t(padc[dil:2 * dil], full[4])
    halo_c()
    gout[:dil, half:] = (low + dot_t(padc[:dil], full[4])).astype(BF16)
    gout[dil:, half:] = (high + dot_t(padc[3 * dil:], full[2])).astype(BF16)
    stores.append(here(gout.at[:, pl.ds(half, half)], grad_in.at[0, 0, :, pl.ds(half, half)]))
    for copy in started:
        copy.wait_send()
    for copy in stores:
        copy.wait()


def solution(mesh):
    n, heads = mesh.shape["seq"], mesh.shape["head"]

    def shards(top, grad, taps, out_w, mix_w, rc_perm):
        relay = n == 4 and heads % 2 == 0 and mix_w.shape[0] % 32 == 0
        if not relay:
            taps = lax.all_gather(taps, "seq", axis=1, tiled=True)
            out_w = lax.all_gather(out_w, "seq", axis=0, tiled=True)
            mix_w = lax.all_gather(mix_w, "seq", axis=0, tiled=True)
        length, half = top.shape[2], top.shape[3] // 2
        block = (length, half)
        copies = 1 + 5 * (taps.shape[0] + 2) + 2 * (heads - 1) + 6
        return pl.pallas_call(
            functools.partial(kernel, n, heads, relay),
            out_shape=[jax.ShapeDtypeStruct(top.shape, BF16)] * 2,
            in_specs=[pl.BlockSpec(memory_space=pl.ANY)] * 5 + [pl.BlockSpec(memory_space=pltpu.VMEM)],
            out_specs=[pl.BlockSpec(memory_space=pl.ANY)] * 2,
            scratch_shapes=[
                pltpu.VMEM((taps.shape[0] + 2, half, half), BF16),
                pltpu.VMEM((half, half), BF16),
                pltpu.VMEM((length, 2 * half), BF16),
                pltpu.VMEM(block, BF16),
                pltpu.VMEM(block, BF16),
                pltpu.VMEM((length, 2 * half), BF16),
                pltpu.VMEM((2 * length, half), BF16),
                pltpu.VMEM((2 * length, half), BF16),
                pltpu.VMEM(block, BF16),
                pltpu.VMEM(block, BF16),
                pltpu.VMEM(block, F32),
                pltpu.VMEM(block, F32),
                pltpu.VMEM((length, 2 * half), BF16),
                pltpu.VMEM((length, 2 * half), BF16),
                pltpu.SemaphoreType.DMA((copies,)),
                pltpu.SemaphoreType.DMA((copies,)),
                pltpu.SemaphoreType.DMA((taps.shape[0] + 8,)),
            ],
            compiler_params=pltpu.CompilerParams(
                collective_id=0, has_side_effects=True, vmem_limit_bytes=56 * 2**20),
            cost_estimate=pl.CostEstimate(
                flops=24 * length * half * half, bytes_accessed=16 * length * half, transcendentals=length * half),
        )(top, grad, taps, out_w, mix_w, rc_perm.reshape(1, half))

    return jax.shard_map(
        lambda *args: tuple(shards(*args)),
        mesh=mesh,
        in_specs=(
            P("head", "strand", "seq", None),
            P(None, "strand", "seq", "head"),
            P(None, "seq", None),
            P("seq", None),
            P("seq", None),
            P(),
        ),
        out_specs=(P("head", "strand", "seq", None), P("head", "strand", "seq", None)),
        check_vma=False,
    )
```

time: 103 us -> 50.9 us (0.49)
  Pallas kernels: 0 us -> 45.8 us
  waiting for transfers between devices: 38.1 us -> 0 us
  starting transfers between devices: 20.3 us -> 0 us
  matrix products: 14.8 us -> 0 us
  between operations: 14.1 us -> 0.65 us
  local copies, waits for them, and re-layouts: 12.8 us -> 4.29 us
  other arithmetic: 2.82 us -> 0 us
    pallas_call x0 -> x1, Pallas kernels: none -> 45.8 us  [shards(): pl.pallas_call(functools.partial(kernel, n, heads, relay), out_shape=[jax...]
    all_gather x3 -> x0, waiting for transfers between devices: 25 us -> none  [the longest x1 12.7 us: shards(): lax.all_gather(out_w, 'seq', axis=0, tiled=True)]
    ppermute x6 -> x0, starting transfers between devices: 14.8 us -> none  [the longest x2 8.14 us: with_halo(): before = lax.ppermute(last, axis, up)]
    dot_general x10 -> x0, matrix products: 14.8 us -> none  [the longest x1 2.51 us: shards(): jnp.einsum('pd,cd->pc', cot_a, out_full, preferred_element_type=jnp.float32)]
    all_to_all x1 -> x0, waiting for transfers between devices: 6.73 us -> none  [shards(): lax.all_to_all(grad_heads, 'head', split_axis=0, concat_axis=3, tiled=True)]
    gather x4 -> x0, local copies, waits for them, and re-layouts: 5.65 us -> none  [the longest x2 2.83 us: shards(): returned = swapped(jnp.take(backed, inverse, axis=1), 'strand', 0)]
    all_to_all x1 -> x0, starting transfers between devices: 5.43 us -> none  [shards(): lax.all_to_all(grad_heads, 'head', split_axis=0, concat_axis=3, tiled=True)]
    ppermute x6 -> x0, waiting for transfers between devices: 5.06 us -> none  [the longest x2 5.05 us: swapped(): return lax.ppermute(value, axis, pairs)]
  transfers between devices with their start and end apart: 10 -> 0, of which waited for: 4 -> 0; matrix products, arithmetic and copies ran while one was open for 24% -> 0% of each run, Pallas kernels for 0% -> 0%
where the time goes in v1:
time: 50.9 us; the launch traced here: 50.7 us
  Pallas kernels  45.8 us (90%)
  local copies, waits for them, and re-layouts  4.29 us (8%)
  between operations  0.65 us (1%)
    pallas_call x1, Pallas kernels, shards(): pl.pallas_call(functools.partial(kernel, n, heads, relay), out_shape=[jax...  45.8 us
    unnamed x4, local copies, waits for them, and re-layouts  3.02 us
    reshape x1, local copies, waits for them, and re-layouts, shards(): rc_perm.reshape(1, half)  1.27 us

profile of v1, /device:TPU:1, one launch (start us, length us, event | category | flops | bytes accessed | tf_op | source)
XLA Modules:
  0.0 50.7 jit_solution(2897451243261572263)
XLA Ops:
  0.6 1.3 %reshape.7.perm = s32[1,768]{1,0:T(1,128)} reshape(s32[768]{0:T(1024)} %param.11) | data formatting | bytes 6144 | tf_op jit(solution)/shard_map/reshape | solution.py:307
  1.9 45.8 %shard_map.77 = (bf16[1,1,256,1536]{3,2,1,0:T(8,128)(2,1)}, bf16[1,1,256,1536]{3,2,1,0:T(8,128)(2,1)}) custom-call(bf16[1,1,256,1536]{3,2,1,0:T(8,128)(2,1)} %top.1, bf16[4,1,256,384]{3,2,1,0:T(8,128)(2,1)} %grad.1, bf16[3,192,768]{2,1,0:T(8,128)(2,1)} %taps.1, bf16[192,768]{1,0:T(8,128)(2,1)} %out_w.1, bf16[192,768]{1,0:T(8,128)(2,1)} %mix_w.1, ...), custom_call_target="tpu_custom_call" | custom-call | flops 3623878656 | bytes 3145728 | tf_op jit(solution)/shard_map/pallas_call | solution.py:279
  47.7 0.0 copy-start
  47.7 2.1 %copy.10 = bf16[1,1,256,1536]{3,2,1,0:T(8,128)(2,1)} copy(bf16[1,1,256,1536]{3,2,1,0:T(8,128)(2,1)} %get-tuple-element.4) | data formatting | bytes 1572864
  49.8 0.0 copy-done
  49.8 0.9 %copy.11 = bf16[1,1,256,1536]{3,2,1,0:T(8,128)(2,1)} copy(bf16[1,1,256,1536]{3,2,1,0:T(8,128)(2,1)S(1)} %copy-done) | data formatting | bytes 1572864
Async XLA Ops:
  47.7 2.1 %copy-start = (bf16[1,1,256,1536]{3,2,1,0:T(8,128)(2,1)S(1)}, bf16[1,1,256,1536]{3,2,1,0:T(8,128)(2,1)}, u32[]{:S(2)}) copy-start(bf16[1,1,256,1536]{3,2,1,0:T(8,128)(2,1)} %get-tuple-element.5) | copy-start | bytes 2359300

commit v2 on v1

--- a/solution.py
+++ b/solution.py
@@ -11,6 +11,10 @@
 MESH = pl.DeviceIdType.MESH
 F32, BF16 = jnp.float32, jnp.bfloat16
 ROUTES = ("far", "strand", "head", "head", "head")
+PARTS = (1, 1, 2, 2, 2)
+PIECES = [(m, k) for m in range(5) for k in range(PARTS[m])]
+AHEAD = 2
+LATE = True
 
 
 def dot(a, b):
@@ -25,7 +29,7 @@
     n, heads, relay,
     top, grad, taps, out_w, mix_w, perm,
     restored, grad_in,
-    full, onehot, topv, other, paired, cot, pad, padc, backed, back_in, pre, pulled, rest, gout,
+    full, onehot, topv, other, paired, cot, pad, padc, backed, back_in, pre, pulled,
     send, recv, local,
 ):
     s, x, z = lax.axis_index("seq"), lax.axis_index("strand"), lax.axis_index("head")
@@ -81,56 +85,68 @@
         core = lax.rem(s, 2)
         sib, far = s + 1 - 2 * core, lax.rem(s + 2, n)
         sib_far = lax.rem(sib + 2, n)
-        hr = rows // 2
-
         def seg(m, owner, first, size):
             return full.at[m, pl.ds(pl.multiple_of(owner * rows + first, 16), size), :]
 
         plans = []
-        for m in range(count):
+        for m, k in PIECES:
+            unit = rows // PARTS[m]
+            hr = unit // 2
             turn = {"far": None, "strand": x, "head": lax.rem(z, 2)}[ROUTES[m]]
-            first, size = (0, rows) if turn is None else (pl.multiple_of(turn * hr, 16), hr)
-            rest_first = None if turn is None else pl.multiple_of((1 - turn) * hr, 16)
+            first, size = (k * unit, unit) if turn is None else (k * unit + turn * hr, hr)
+            other_half = None if turn is None else k * unit + (1 - turn) * hr
             partner = {"far": None, "strand": to_strand, "head": {"head": z + 1 - 2 * lax.rem(z, 2)}}[ROUTES[m]]
             w = weights[m]
             plan = {
-                "first": first, "size": size, "rest": rest_first,
-                "sib": remote(w, seg(m, s, 0, rows), {"seq": sib}),
+                "first": first, "size": size, "rest": other_half, "hr": hr, "unit": unit,
+                "sib": remote(w.at[pl.ds(k * unit, unit), :], seg(m, s, k * unit, unit), {"seq": sib}),
                 "far": remote(w.at[pl.ds(first, size), :], seg(m, s, first, size), {"seq": far}),
                 "fwd": remote(seg(m, far, first, size), seg(m, far, first, size), {"seq": sib}),
             }
             if turn is not None:
                 plan["relay"] = remote(seg(m, far, first, size), seg(m, far, first, size), partner)
-                plan["fwd2"] = remote(seg(m, far, rest_first, hr), seg(m, far, rest_first, hr), {"seq": sib})
+                plan["fwd2"] = remote(seg(m, far, other_half, hr), seg(m, far, other_half, hr), {"seq": sib})
             plans.append(plan)
 
-    def push(m):
+    def push(i):
+        if relay and i < len(PIECES):
+            start(plans[i]["far"])
+            start(plans[i]["sib"])
+
+    def piece_a(i):
         if relay:
-            start(plans[m]["far"])
-            start(plans[m]["sib"])
-
-    def stage_a(m):
-        if relay:
-            p = plans[m]
+            p, m = plans[i], PIECES[i][0]
             arrived(p["far"], seg(m, far, p["first"], p["size"]))
+            push(i + AHEAD)
             if p["rest"] is not None:
                 start(p["relay"])
             start(p["fwd"])
 
-    def stage_b(m):
-        if relay and plans[m]["rest"] is not None:
-            p = plans[m]
-            arrived(p["relay"], seg(m, far, p["rest"], hr))
+    def piece_b(i):
+        if relay and plans[i]["rest"] is not None:
+            p, m = plans[i], PIECES[i][0]
+            arrived(p["relay"], seg(m, far, p["rest"], p["hr"]))
             start(p["fwd2"])
 
-    def stage_c(m):
-        own_w[m].wait()
+    def piece_c(i):
+        m, k = PIECES[i]
+        if k == 0:
+            own_w[m].wait()
         if relay:
-            p = plans[m]
-            arrived(p["sib"], seg(m, sib, 0, rows))
+            p = plans[i]
+            arrived(p["sib"], seg(m, sib, k * p["unit"], p["unit"]))
             arrived(p["fwd"], seg(m, sib_far, p["first"], p["size"]))
             if p["rest"] is not None:
-                arrived(p["fwd2"], seg(m, sib_far, p["rest"], hr))
+                arrived(p["fwd2"], seg(m, sib_far, p["rest"], p["hr"]))
+
+    def each(stage, m):
+        for i, (owner, _) in enumerate(PIECES):
+            if owner == m:
+                stage(i)
+
+    stage_a = functools.partial(each, piece_a)
+    stage_b = functools.partial(each, piece_b)
+    stage_c = functools.partial(each, piece_c)
 
     def piece(h, owner):
         return cot.at[pl.ds(h * dil, dil), pl.ds(pl.multiple_of(owner * width, 128), width)]
@@ -144,13 +160,14 @@
     push(0)
     for make in gifts[0]:
         start(make)
-    for m in range(1, count):
-        push(m)
-    for make in gifts[1]:
-        start(make)
+    for i in range(1, AHEAD):
+        push(i)
+    if not LATE:
+        for make in gifts[1]:
+            start(make)
 
     index = lax.broadcasted_iota(jnp.int32, (half, half), 0)
-    onehot[...] = jnp.where(index == perm[...], 1.0, 0.0).astype(BF16)
+    onehot[...] = jnp.where(index == perm[...].reshape(1, half), 1.0, 0.0).astype(BF16)
 
     @pl.when(s == 0)
     def _():
@@ -164,6 +181,9 @@
 
     top_copy.wait()
     arrived(swap, other)
+    if LATE:
+        for make in gifts[1]:
+            start(make)
     paired[...] = (topv[:, :half].astype(F32) + dot(other[...], onehot[...])).astype(BF16)
 
     def halo(buf):
@@ -209,9 +229,8 @@
     stage_c(0)
     input_b = (topv[:, half:].astype(F32) - dot(paired[...], full[0])).astype(BF16)
     pad[dil:3 * dil] = input_b
-    rest[:, half:] = input_b
+    restored[0, 0, :, half:] = input_b
     halo_b = halo(pad)
-    stores = [here(rest.at[:, pl.ds(half, half)], restored.at[0, 0, :, pl.ds(half, half)])]
     back(0)
     stage_a(2)
     stage_b(1)
@@ -221,8 +240,8 @@
     stage_b(2)
     stage_c(2)
     pre[...] = dot(pad[0:2 * dil], full[2])
+    stage_a(4)
     back(1)
-    stage_a(4)
     stage_b(3)
     stage_c(3)
     pre[...] += dot(pad[dil:3 * dil], full[3])
@@ -232,9 +251,8 @@
         arrived(returns[h], back_in.at[pl.ds(h * dil, dil)])
         returned = dot_t(back_in[rows_h], onehot[...])
         cot_a = (cot[rows_h, :half].astype(F32) + backed[rows_h].astype(F32) + returned).astype(BF16)
-        gout[rows_h, :half] = cot_a
+        grad_in[0, 0, rows_h, :half] = cot_a
         pulled[rows_h] = dot_t(cot_a, full[1])
-    stores.append(here(gout.at[:, pl.ds(0, half)], grad_in.at[0, 0, :, pl.ds(0, half)]))
 
     stage_b(4)
     stage_c(4)
@@ -249,18 +267,25 @@
         padc[(1 + h) * dil:(2 + h) * dil] = (pulled[rows_h] * slope).astype(BF16)
         paired[rows_h] = (v * cdf).astype(BF16)
     halo_c = halo(padc)
-    rest[:, :half] = (topv[:, :half].astype(F32) - dot(paired[...], full[1])).astype(BF16)
-    stores.append(here(rest.at[:, pl.ds(0, half)], restored.at[0, 0, :, pl.ds(0, half)]))
+    restored[0, 0, :, :half] = (topv[:, :half].astype(F32) - dot(paired[...], full[1])).astype(BF16)
     total = cot[:, half:].astype(F32) + dot_t(padc[dil:3 * dil], full[3])
     low = total[:dil] + dot_t(padc[2 * dil:3 * dil], full[2])
     high = total[dil:] + dot_t(padc[dil:2 * dil], full[4])
     halo_c()
-    gout[:dil, half:] = (low + dot_t(padc[:dil], full[4])).astype(BF16)
-    gout[dil:, half:] = (high + dot_t(padc[3 * dil:], full[2])).astype(BF16)
-    stores.append(here(gout.at[:, pl.ds(half, half)], grad_in.at[0, 0, :, pl.ds(half, half)]))
+    grad_in[0, 0, :dil, half:] = (low + dot_t(padc[:dil], full[4])).astype(BF16)
+    grad_in[0, 0, dil:, half:] = (high + dot_t(padc[3 * dil:], full[2])).astype(BF16)
     for copy in started:
         copy.wait_send()
-    for copy in stores:
+
+
+def write_out(restored, grad_in, restored_out, grad_out, sem):
+    copies = [
+        pltpu.make_async_copy(restored, restored_out, sem.at[0]),
+        pltpu.make_async_copy(grad_in, grad_out, sem.at[1]),
+    ]
+    for copy in copies:
+        copy.start()
+    for copy in copies:
         copy.wait()
 
 
@@ -275,12 +300,12 @@
             mix_w = lax.all_gather(mix_w, "seq", axis=0, tiled=True)
         length, half = top.shape[2], top.shape[3] // 2
         block = (length, half)
-        copies = 1 + 5 * (taps.shape[0] + 2) + 2 * (heads - 1) + 6
-        return pl.pallas_call(
+        copies = 1 + 5 * len(PIECES) + 2 * (heads - 1) + 6
+        found = pl.pallas_call(
             functools.partial(kernel, n, heads, relay),
-            out_shape=[jax.ShapeDtypeStruct(top.shape, BF16)] * 2,
+            out_shape=[pltpu.VMEM(top.shape, BF16)] * 2,
             in_specs=[pl.BlockSpec(memory_space=pl.ANY)] * 5 + [pl.BlockSpec(memory_space=pltpu.VMEM)],
-            out_specs=[pl.BlockSpec(memory_space=pl.ANY)] * 2,
+            out_specs=[pl.BlockSpec(memory_space=pltpu.VMEM)] * 2,
             scratch_shapes=[
                 pltpu.VMEM((taps.shape[0] + 2, half, half), BF16),
                 pltpu.VMEM((half, half), BF16),
@@ -294,8 +319,6 @@
                 pltpu.VMEM(block, BF16),
                 pltpu.VMEM(block, F32),
                 pltpu.VMEM(block, F32),
-                pltpu.VMEM((length, 2 * half), BF16),
-                pltpu.VMEM((length, 2 * half), BF16),
                 pltpu.SemaphoreType.DMA((copies,)),
                 pltpu.SemaphoreType.DMA((copies,)),
                 pltpu.SemaphoreType.DMA((taps.shape[0] + 8,)),
@@ -304,7 +327,14 @@
                 collective_id=0, has_side_effects=True, vmem_limit_bytes=56 * 2**20),
             cost_estimate=pl.CostEstimate(
                 flops=24 * length * half * half, bytes_accessed=16 * length * half, transcendentals=length * half),
-        )(top, grad, taps, out_w, mix_w, rc_perm.reshape(1, half))
+        )(top, grad, taps, out_w, mix_w, rc_perm)
+        return pl.pallas_call(
+            write_out,
+            out_shape=[jax.ShapeDtypeStruct(top.shape, BF16)] * 2,
+            in_specs=[pl.BlockSpec(memory_space=pltpu.VMEM)] * 2,
+            out_specs=[pl.BlockSpec(memory_space=pl.ANY)] * 2,
+            scratch_shapes=[pltpu.SemaphoreType.DMA((2,))],
+        )(*[pltpu.with_memory_space_constraint(f, pltpu.VMEM) for f in found])
 
     return jax.shard_map(
         lambda *args: tuple(shards(*args)),

time: 50.9 us -> 46.2 us (0.908)
  local copies, waits for them, and re-layouts: 4.29 us -> 0 us
    unnamed x4 -> x0, local copies, waits for them, and re-layouts: 3.02 us -> none
    reshape x1 -> x0, local copies, waits for them, and re-layouts: 1.27 us -> none  [shards(): rc_perm.reshape(1, half)]
    pallas_call x1 -> x2, Pallas kernels: 45.8 us -> 45.4 us  [the longest x1 44.3 us: shards(): pl.pallas_call(functools.partial(kernel, n, heads, relay), out_shape=[plt...]
where the time goes in v2:
time: 46.2 us; the launch traced here: 46.1 us
  Pallas kernels  45.4 us (98%)
  between operations  0.64 us (1%)
    pallas_call x1, Pallas kernels, shards(): pl.pallas_call(functools.partial(kernel, n, heads, relay), out_shape=[plt...  44.3 us
    pallas_call x1, Pallas kernels, shards(): pl.pallas_call(write_out, out_shape=[jax.ShapeDtypeStruct(top.shape, BF16...  1.16 us

profile of v2, /device:TPU:1, one launch (start us, length us, event | category | flops | bytes accessed | tf_op | source)
XLA Modules:
  0.0 46.1 jit_solution(16388330698638332763)
XLA Ops:
  0.6 44.3 %shard_map.77 = (bf16[1,1,256,1536]{3,2,1,0:T(8,128)(2,1)S(1)}, bf16[1,1,256,1536]{3,2,1,0:T(8,128)(2,1)S(1)}) custom-call(bf16[1,1,256,1536]{3,2,1,0:T(8,128)(2,1)} %top.1, bf16[4,1,256,384]{3,2,1,0:T(8,128)(2,1)} %grad.1, bf16[3,192,768]{2,1,0:T(8,128)(2,1)} %taps.1, bf16[192,768]{1,0:T(8,128)(2,1)} %out_w.1, bf16[192,768]{1,0:T(8,128)(2,1)} %mix_w.1, ...), custom_call_target="tpu_custom_call" | custom-call | flops 3623878656 | bytes 3145728 | tf_op jit(solution)/shard_map/pallas_call | solution.py:304
  44.9 1.2 %shard_map.78 = (bf16[1,1,256,1536]{3,2,1,0:T(8,128)(2,1)}, bf16[1,1,256,1536]{3,2,1,0:T(8,128)(2,1)}) custom-call(bf16[1,1,256,1536]{3,2,1,0:T(8,128)(2,1)S(1)} %get-tuple-element.4.restored, bf16[1,1,256,1536]{3,2,1,0:T(8,128)(2,1)S(1)} %get-tuple-element.5.grad_in), custom_call_target="tpu_custom_call" | custom-call | tf_op jit(solution)/shard_map/pallas_call | solution.py:331

commit v3 on v2

--- a/solution.py
+++ b/solution.py
@@ -10,9 +10,10 @@
 
 MESH = pl.DeviceIdType.MESH
 F32, BF16 = jnp.float32, jnp.bfloat16
-ROUTES = ("far", "strand", "head", "head", "head")
-PARTS = (1, 1, 2, 2, 2)
-PIECES = [(m, k) for m in range(5) for k in range(PARTS[m])]
+ROUTES = ('far', 'head', 'strand', 'head', 'head')
+PARTS = (1, 1, 1, 1, 1)
+ORDER = (0, 2, 3, 4, 1)
+PIECES = [(m, k) for m in ORDER for k in range(PARTS[m])]
 AHEAD = 2
 LATE = True
 
@@ -29,7 +30,7 @@
     n, heads, relay,
     top, grad, taps, out_w, mix_w, perm,
     restored, grad_in,
-    full, onehot, topv, other, paired, cot, pad, padc, backed, back_in, pre, pulled,
+    full, onehot, topv, other, paired, cot, pad, padc, backed, back_in, pre, slope,
     send, recv, local,
 ):
     s, x, z = lax.axis_index("seq"), lax.axis_index("strand"), lax.axis_index("head")
@@ -111,7 +112,6 @@
     def push(i):
         if relay and i < len(PIECES):
             start(plans[i]["far"])
-            start(plans[i]["sib"])
 
     def piece_a(i):
         if relay:
@@ -128,13 +128,18 @@
             arrived(p["relay"], seg(m, far, p["rest"], p["hr"]))
             start(p["fwd2"])
 
-    def piece_c(i):
+    def piece_near(i):
         m, k = PIECES[i]
         if k == 0:
             own_w[m].wait()
         if relay:
             p = plans[i]
             arrived(p["sib"], seg(m, sib, k * p["unit"], p["unit"]))
+
+    def piece_c(i):
+        m, k = PIECES[i]
+        if relay:
+            p = plans[i]
             arrived(p["fwd"], seg(m, sib_far, p["first"], p["size"]))
             if p["rest"] is not None:
                 arrived(p["fwd2"], seg(m, sib_far, p["rest"], p["hr"]))
@@ -146,7 +151,12 @@
 
     stage_a = functools.partial(each, piece_a)
     stage_b = functools.partial(each, piece_b)
-    stage_c = functools.partial(each, piece_c)
+    stage_near = functools.partial(each, piece_near)
+    stage_far = functools.partial(each, piece_c)
+
+    def stage_c(m):
+        stage_near(m)
+        stage_far(m)
 
     def piece(h, owner):
         return cot.at[pl.ds(h * dil, dil), pl.ds(pl.multiple_of(owner * width, 128), width)]
@@ -162,6 +172,9 @@
         start(make)
     for i in range(1, AHEAD):
         push(i)
+    if relay:
+        for p in plans:
+            start(p["sib"])
     if not LATE:
         for make in gifts[1]:
             start(make)
@@ -186,9 +199,12 @@
             start(make)
     paired[...] = (topv[:, :half].astype(F32) + dot(other[...], onehot[...])).astype(BF16)
 
-    def halo(buf):
-        up = remote(buf.at[pl.ds(2 * dil, dil)], buf.at[pl.ds(0, dil)], {"seq": lax.rem(s + 1, n)})
-        down = remote(buf.at[pl.ds(dil, dil)], buf.at[pl.ds(3 * dil, dil)], {"seq": lax.rem(s + n - 1, n)})
+    def halo(buf, cols):
+        def rows_at(i):
+            return buf.at[pl.ds(i * dil, dil), cols]
+
+        up = remote(rows_at(2), rows_at(0), {"seq": lax.rem(s + 1, n)})
+        down = remote(rows_at(1), rows_at(3), {"seq": lax.rem(s + n - 1, n)})
 
         @pl.when(s < n - 1)
         def _():
@@ -201,12 +217,12 @@
         def finish():
             @pl.when(s > 0)
             def _():
-                arrived(up, buf.at[pl.ds(0, dil)])
+                arrived(up, rows_at(0))
                 down().wait_send()
 
             @pl.when(s < n - 1)
             def _():
-                arrived(down, buf.at[pl.ds(3 * dil, dil)])
+                arrived(down, rows_at(3))
                 up().wait_send()
 
         return finish
@@ -224,37 +240,26 @@
         start(returns[h])
 
     stage_a(0)
-    stage_a(1)
+    stage_a(2)
     stage_b(0)
     stage_c(0)
     input_b = (topv[:, half:].astype(F32) - dot(paired[...], full[0])).astype(BF16)
     pad[dil:3 * dil] = input_b
+    halo_b = halo(pad, pl.ds(0, half))
     restored[0, 0, :, half:] = input_b
-    halo_b = halo(pad)
     back(0)
-    stage_a(2)
-    stage_b(1)
-    stage_c(1)
-    halo_b()
     stage_a(3)
     stage_b(2)
     stage_c(2)
+    halo_b()
     pre[...] = dot(pad[0:2 * dil], full[2])
     stage_a(4)
     back(1)
     stage_b(3)
     stage_c(3)
     pre[...] += dot(pad[dil:3 * dil], full[3])
-
-    for h in range(2):
-        rows_h = slice(h * dil, (h + 1) * dil)
-        arrived(returns[h], back_in.at[pl.ds(h * dil, dil)])
-        returned = dot_t(back_in[rows_h], onehot[...])
-        cot_a = (cot[rows_h, :half].astype(F32) + backed[rows_h].astype(F32) + returned).astype(BF16)
-        grad_in[0, 0, rows_h, :half] = cot_a
-        pulled[rows_h] = dot_t(cot_a, full[1])
-
     stage_b(4)
+    stage_a(1)
     stage_c(4)
     scale = math.sqrt(2.0 / math.pi)
     for h in range(2):
@@ -263,17 +268,46 @@
         square = v * v
         t = jnp.tanh(scale * (v + 0.044715 * (square * v)))
         cdf = 0.5 * (1.0 + t)
-        slope = cdf + 0.5 * v * (1.0 - t * t) * (scale * (1.0 + 3 * 0.044715 * square))
-        padc[(1 + h) * dil:(2 + h) * dil] = (pulled[rows_h] * slope).astype(BF16)
+        slope[rows_h] = cdf + 0.5 * v * (1.0 - t * t) * (scale * (1.0 + 3 * 0.044715 * square))
         paired[rows_h] = (v * cdf).astype(BF16)
-    halo_c = halo(padc)
+
+    for h in range(2):
+        rows_h = slice(h * dil, (h + 1) * dil)
+        arrived(returns[h], back_in.at[pl.ds(h * dil, dil)])
+        returned = dot_t(back_in[rows_h], onehot[...])
+        grad_in[0, 0, rows_h, :half] = (
+            cot[rows_h, :half].astype(F32) + backed[rows_h].astype(F32) + returned).astype(BF16)
+
+    near = s // 2 if relay else 0
+    parts = [pl.ds(pl.multiple_of(c * (half // 2), 128), half // 2) for c in (near, 1 - near)]
+
+    def columns(cols):
+        pulled = dot_t(grad_in[0, 0, :, :half], full[1, cols, :])
+        padc[dil:3 * dil, cols] = (pulled * slope[:, cols]).astype(BF16)
+        return halo(padc, cols)
+
+    def inner(cols):
+        pre[...] += dot_t(padc[dil:3 * dil, cols], full[3, :, cols])
+        pre[:dil] += dot_t(padc[2 * dil:3 * dil, cols], full[2, :, cols])
+        pre[dil:] += dot_t(padc[dil:2 * dil, cols], full[4, :, cols])
+
+    def edges(cols):
+        return (dot_t(padc[:dil, cols], full[4, :, cols]), dot_t(padc[3 * dil:, cols], full[2, :, cols]))
+
+    stage_near(1)
+    halo_near = columns(parts[0])
+    pre[...] = cot[:, half:].astype(F32)
+    inner(parts[0])
+    stage_b(1)
+    stage_far(1)
+    halo_far = columns(parts[1])
+    inner(parts[1])
     restored[0, 0, :, :half] = (topv[:, :half].astype(F32) - dot(paired[...], full[1])).astype(BF16)
-    total = cot[:, half:].astype(F32) + dot_t(padc[dil:3 * dil], full[3])
-    low = total[:dil] + dot_t(padc[2 * dil:3 * dil], full[2])
-    high = total[dil:] + dot_t(padc[dil:2 * dil], full[4])
-    halo_c()
-    grad_in[0, 0, :dil, half:] = (low + dot_t(padc[:dil], full[4])).astype(BF16)
-    grad_in[0, 0, dil:, half:] = (high + dot_t(padc[3 * dil:], full[2])).astype(BF16)
+    halo_near()
+    halo_far()
+    low, high = edges(slice(None))
+    grad_in[0, 0, :dil, half:] = (pre[:dil] + low).astype(BF16)
+    grad_in[0, 0, dil:, half:] = (pre[dil:] + high).astype(BF16)
     for copy in started:
         copy.wait_send()
 
@@ -300,7 +334,7 @@
             mix_w = lax.all_gather(mix_w, "seq", axis=0, tiled=True)
         length, half = top.shape[2], top.shape[3] // 2
         block = (length, half)
-        copies = 1 + 5 * len(PIECES) + 2 * (heads - 1) + 6
+        copies = 1 + 5 * len(PIECES) + 2 * (heads - 1) + 8
         found = pl.pallas_call(
             functools.partial(kernel, n, heads, relay),
             out_shape=[pltpu.VMEM(top.shape, BF16)] * 2,

time: 46.2 us -> 43.8 us (0.948)
  Pallas kernels: 45.4 us -> 43 us
    pallas_call x1, Pallas kernels: 44.3 us -> 41.8 us  [shards(): pl.pallas_call(functools.partial(kernel, n, heads, relay), out_shape=[plt...]
where the time goes in v3:
time: 43.8 us; the launch traced here: 43.6 us
  Pallas kernels  43 us (98%)
  between operations  0.64 us (1%)
    pallas_call x1, Pallas kernels, shards(): pl.pallas_call(functools.partial(kernel, n, heads, relay), out_shape=[plt...  41.8 us
    pallas_call x1, Pallas kernels, shards(): pl.pallas_call(write_out, out_shape=[jax.ShapeDtypeStruct(top.shape, BF16...  1.16 us

profile of v3, /device:TPU:1, one launch (start us, length us, event | category | flops | bytes accessed | tf_op | source)
XLA Modules:
  0.0 43.6 jit_solution(6737520965443686042)
XLA Ops:
  0.6 41.8 %shard_map.77 = (bf16[1,1,256,1536]{3,2,1,0:T(8,128)(2,1)S(1)}, bf16[1,1,256,1536]{3,2,1,0:T(8,128)(2,1)S(1)}) custom-call(bf16[1,1,256,1536]{3,2,1,0:T(8,128)(2,1)} %top.1, bf16[4,1,256,384]{3,2,1,0:T(8,128)(2,1)} %grad.1, bf16[3,192,768]{2,1,0:T(8,128)(2,1)} %taps.1, bf16[192,768]{1,0:T(8,128)(2,1)} %out_w.1, bf16[192,768]{1,0:T(8,128)(2,1)} %mix_w.1, ...), custom_call_target="tpu_custom_call" | custom-call | flops 3623878656 | bytes 3145728 | tf_op jit(solution)/shard_map/pallas_call | solution.py:338
  42.4 1.2 %shard_map.78 = (bf16[1,1,256,1536]{3,2,1,0:T(8,128)(2,1)}, bf16[1,1,256,1536]{3,2,1,0:T(8,128)(2,1)}) custom-call(bf16[1,1,256,1536]{3,2,1,0:T(8,128)(2,1)S(1)} %get-tuple-element.4.restored, bf16[1,1,256,1536]{3,2,1,0:T(8,128)(2,1)S(1)} %get-tuple-element.5.grad_in), custom_call_target="tpu_custom_call" | custom-call | tf_op jit(solution)/shard_map/pallas_call | solution.py:365
